TPU v7x, 128 devices: a whole 4x4x4 slice. The times are simulated.
128 devices in a mesh: frames: 16 (over x, z), codes: 8 (over y, core).
Axes of the slice: x: 4, y: 4, z: 4, core: 2. Of those that a mesh axis runs over, the one named last changes fastest.
Arguments:
- features: bfloat16 [32768, 128], P('frames'), may hold values from -500 to 500
- codebook: bfloat16 [65536, 128], P(('codes', 'frames')), may hold values from -50 to 50
- tile_count: int32 [256, 8], P('frames', 'codes'), may hold values from 1 to 16, as said below
- tile_cols: int32 [256, 8, 16], P('frames', 'codes'), may hold values from 0 to 63, as said below
Outputs:
- quantized: float32 [32768, 128], P(('frames', 'codes'))
- col_log_scale: float32 [65536], P(('codes', 'frames'))
Inputs may be any that keep to these rules, and one draw needn't show every extreme that they name: `tile_count`: for every tile row the counts over the 8 blocks sum to 64, and exactly one block of the row has 16. `tile_cols`: the first tile_count entries of a tile row and block are distinct; entries from tile_count on are ignored. Every column tile of the whole is live in some tile row.
All inputs are finite; a program needn't handle non-finite values.
Results may differ from a plain program's by a relative error of at most 0.0009.
Values may be sent and summed in bfloat16 or wider, within the bound.
A program may use at most 128 MiB of HBM per device.

v0:
```python
import math

import jax
import jax.numpy as jnp
from jax import lax
from jax.sharding import PartitionSpec as P

ITERS = 4


EPS = 1e-06
INV_TEMP = 10.0


def per_device(features, codebook, tile_count, tile_cols):
    high = lax.Precision.HIGHEST
    frame_rows, embed = features.shape
    row_tiles = tile_cols.shape[0]
    tile = frame_rows // row_tiles
    codebook_all = lax.all_gather(codebook, "frames", axis=0, tiled=True)
    code_rows = codebook_all.shape[0]
    col_tiles = code_rows // tile
    frame_groups = lax.axis_size("frames")
    code_groups = lax.axis_size("codes")
    target = frame_rows * frame_groups / (code_rows * code_groups)
    feat_scale = lax.rsqrt(
        jnp.mean(jnp.square(features.astype(jnp.float32)), axis=-1) + EPS
    ).reshape(row_tiles, tile)
    code_scale = lax.rsqrt(
        jnp.mean(jnp.square(codebook_all.astype(jnp.float32)), axis=-1) + EPS
    ).reshape(col_tiles, tile)
    book_tiles = codebook_all.reshape(col_tiles, tile, embed)
    feat_tiles = features.reshape(row_tiles, tile, embed)
    columns = tile_cols[:, 0, :]
    slot_live = (lax.broadcasted_iota(jnp.int32, columns.shape, 1) < tile_count).astype(jnp.float32)
    group = math.gcd(8, row_tiles)

    def kernel_block(first, length):
        feat_block = lax.dynamic_slice_in_dim(feat_tiles, first, length, 0)
        scale_block = lax.dynamic_slice_in_dim(feat_scale, first, length, 0)
        index_block = lax.dynamic_slice_in_dim(columns, first, length, 0)
        live_block = lax.dynamic_slice_in_dim(slot_live, first, length, 0)
        picked = jnp.take(book_tiles, index_block, axis=0)
        products = jnp.einsum(
            "rfe,rske->rsfk", feat_block, picked, preferred_element_type=jnp.float32
        )
        scaled = (
            INV_TEMP
            / embed
            * products
            * scale_block[:, None, :, None]
            * jnp.take(code_scale, index_block, axis=0)[:, :, None, :]
        )
        return (jnp.exp(scaled) * live_block[:, :, None, None], index_block, picked)

    v_tiles = jnp.ones((col_tiles, tile), jnp.float32)
    u_tiles = jnp.ones((row_tiles, tile), jnp.float32)
    own_scale = jnp.ones((code_rows // frame_groups,), jnp.float32)
    v_flat = jnp.ones((code_rows,), jnp.float32)
    for sweep in range(ITERS):
        v_half = v_tiles.astype(jnp.bfloat16)

        def row_visit(turn, acc):
            first = turn * group
            kernel, index_block, picked = kernel_block(first, group)
            kernel_half = kernel.astype(jnp.bfloat16)
            chosen = jnp.take(v_half, index_block, axis=0)
            sums = jnp.einsum(
                "rsfk,rsk->rf", kernel_half, chosen, preferred_element_type=jnp.float32
            )
            return lax.dynamic_update_slice_in_dim(acc, sums, first, 0)

        partial_rows = lax.fori_loop(
            0, row_tiles // group, row_visit, jnp.zeros((row_tiles, tile), jnp.float32)
        )
        u_tiles = 1.0 / lax.psum(partial_rows, "codes")
        u_half = u_tiles.astype(jnp.bfloat16)

        def col_visit(turn, acc):
            first = turn * group
            kernel, index_block, picked = kernel_block(first, group)
            kernel_half = kernel.astype(jnp.bfloat16)
            u_block = lax.dynamic_slice_in_dim(u_half, first, group, 0)
            contrib = jnp.einsum(
                "rsfk,rf->rsk", kernel_half, u_block, preferred_element_type=jnp.float32
            )
            onehot = (
                index_block[:, :, None] == lax.broadcasted_iota(jnp.int32, (1, 1, col_tiles), 2)
            ).astype(jnp.float32)
            return acc + jnp.einsum("rsc,rsk->ck", onehot, contrib, precision=high)

        partial_cols = lax.fori_loop(
            0, row_tiles // group, col_visit, jnp.zeros((col_tiles, tile), jnp.float32)
        ).reshape(code_rows)
        totals = lax.psum(partial_cols, "frames")
        v_flat = target / totals
        share = code_rows // frame_groups
        own_scale = lax.dynamic_slice_in_dim(v_flat, lax.axis_index("frames") * share, share)
        v_tiles = v_flat.reshape(col_tiles, tile)
    count = frame_rows // code_groups * lax.axis_size("codes")
    span = count // tile
    local_group = math.gcd(group, span)

    def mix_visit(turn, acc):
        first = turn * local_group
        kernel, index_block, picked = kernel_block(first, local_group)
        scales = jnp.take(v_tiles, index_block, axis=0)
        weights = (kernel * scales[:, :, None, :]).astype(jnp.bfloat16)
        mixed = jnp.einsum("rsfk,rske->rfe", weights, picked, preferred_element_type=jnp.float32)
        u_block = lax.dynamic_slice_in_dim(u_tiles, first, local_group, 0)
        mixed = (mixed * u_block[:, :, None]).reshape(local_group * tile, embed)
        return lax.dynamic_update_slice_in_dim(acc, mixed, turn * local_group * tile, 0)

    quantized = lax.psum_scatter(
        lax.fori_loop(0, span // local_group, mix_visit, jnp.zeros((count, embed), jnp.float32)),
        "codes",
        scatter_dimension=0,
        tiled=True,
    )
    return (quantized, jnp.log(own_scale))


def solution(mesh):
    return jax.shard_map(
        per_device,
        mesh=mesh,
        in_specs=(
            P("frames", None),
            P(("codes", "frames"), None),
            P("frames", "codes"),
            P("frames", "codes", None),
        ),
        out_specs=(P(("frames", "codes"), None), P(("codes", "frames"))),
        check_vma=False,
    )
```

profile of v0, /device:TPU:1, one launch (start us, length us, event | category | flops | bytes accessed | tf_op | source)
XLA Modules:
  0.0 642.4 jit_solution(2100353860892811804)
XLA Ops:
  10.1 47.5 %all-gather.2.cloned.1.call-done = bf16[8192,128]{1,0:T(8,128)(2,1)} async-done(((bf16[512,128]{1,0:T(8,128)(2,1)}), bf16[8192,128]{1,0:T(8,128)(2,1)}) %all-gather.2.cloned.1.call-update) | async-done | bytes 2097168 | tf_op jit(solution)/shard_map/all_gather | solution.py:20
  60.4 24.2 %while.123 = (s32[]{:T(128)}, f32[16,128]{1,0:T(8,128)S(1)}, s32[16,16]{1,0:T(8,128)}, bf16[64,128,128]{2,1,0:T(8,128)(2,1)}, bf16[16,128,128]{2,1,0:T(8,128)(2,...) while((s32[]{:T(128)}, f32[16,128]{1,0:T(8,128)S(1)}, ...), condition=%wide.region_3.7_spmd, body=%wide.region_2.6_spmd.sunk | while | flops 551586560 | bytes 15489629 | solution.py:73
  67.5 5.0 fusion.261
  79.5 5.0 fusion.261
  84.6 13.7 %psum.56 = f32[16,128]{1,0:T(8,128)S(1)} all-reduce(f32[16,128]{1,0:T(8,128)S(1)} %get-tuple-element.1464), channel_id=1, replica_groups=mesh['frames'=16,'codes'=8] {'codes'}, use_global_device_ids=true, to_apply=%region_4.8 | all-reduce | flops 2048 | bytes 16384 | tf_op jit(solution)/shard_map/psum | solution.py:76
  98.3 23.1 %while.128 = (s32[]{:T(128)}, f32[64,128]{1,0:T(8,128)S(1)}, s32[16,16]{1,0:T(8,128)}, bf16[64,128,128]{2,1,0:T(8,128)(2,1)}, bf16[16,128,128]{2,1,0:T(8,128)(2,...) while((s32[]{:T(128)}, f32[64,128]{1,0:T(8,128)S(1)}, ...), condition=%wide.region_6.10_spmd.clone, body=%wide.region_5.9_spmd.clone.sunk | while | flops 564178048 | bytes 15500781 | solution.py:92
  116.1 4.9 fusion.285
  121.4 58.0 %psum.57 = f32[8192]{0:T(1024)S(1)} all-reduce(f32[8192]{0:T(1024)S(1)} %bitcast.357), channel_id=1, replica_groups=mesh['frames'=16,'codes'=8] {'frames'}, use_global_device_ids=true, to_apply=%region_7.11 | all-reduce | flops 8192 | bytes 65536 | tf_op jit(solution)/shard_map/psum | solution.py:95
  179.5 24.2 %while.124 = (s32[]{:T(128)}, f32[16,128]{1,0:T(8,128)S(1)}, s32[16,16]{1,0:T(8,128)}, bf16[64,128,128]{2,1,0:T(8,128)(2,1)}, bf16[16,128,128]{2,1,0:T(8,128)(2,...) while((s32[]{:T(128)}, f32[16,128]{1,0:T(8,128)S(1)}, ...), condition=%wide.region_9.13_spmd, body=%wide.region_8.12_spmd.sunk | while | flops 551586560 | bytes 15473243 | solution.py:73
  186.5 5.0 fusion.266
  198.6 5.0 fusion.266
  203.6 28.0 %psum.58 = f32[16,128]{1,0:T(8,128)S(1)} all-reduce(f32[16,128]{1,0:T(8,128)S(1)} %get-tuple-element.1466), channel_id=1, replica_groups=mesh['frames'=16,'codes'=8] {'codes'}, use_global_device_ids=true, to_apply=%region_10.14 | all-reduce | flops 2048 | bytes 16384 | tf_op jit(solution)/shard_map/psum | solution.py:76
  231.7 23.1 %while.129 = (s32[]{:T(128)}, f32[64,128]{1,0:T(8,128)S(1)}, s32[16,16]{1,0:T(8,128)}, bf16[64,128,128]{2,1,0:T(8,128)(2,1)}, bf16[16,128,128]{2,1,0:T(8,128)(2,...) while((s32[]{:T(128)}, f32[64,128]{1,0:T(8,128)S(1)}, ...), condition=%wide.region_12.16_spmd.clone, body=%wide.region_11.15_spmd.clone.sunk | while | flops 564178048 | bytes 15500781 | solution.py:92
  238.0 4.9 fusion.292
  254.8 56.3 %psum.59 = f32[8192]{0:T(1024)S(1)} all-reduce(f32[8192]{0:T(1024)S(1)} %bitcast.356), channel_id=1, replica_groups=mesh['frames'=16,'codes'=8] {'frames'}, use_global_device_ids=true, to_apply=%region_13.17 | all-reduce | flops 8192 | bytes 65536 | tf_op jit(solution)/shard_map/psum | solution.py:95
  311.2 24.2 %while.125 = (s32[]{:T(128)}, f32[16,128]{1,0:T(8,128)S(1)}, s32[16,16]{1,0:T(8,128)}, bf16[64,128,128]{2,1,0:T(8,128)(2,1)}, bf16[16,128,128]{2,1,0:T(8,128)(2,...) while((s32[]{:T(128)}, f32[16,128]{1,0:T(8,128)S(1)}, ...), condition=%wide.region_15.19_spmd, body=%wide.region_14.18_spmd.sunk | while | flops 551586560 | bytes 15473243 | solution.py:73
  318.2 5.0 fusion.271
  330.3 5.0 fusion.271
  335.3 25.9 %psum.60 = f32[16,128]{1,0:T(8,128)S(1)} all-reduce(f32[16,128]{1,0:T(8,128)S(1)} %get-tuple-element.1468), channel_id=1, replica_groups=mesh['frames'=16,'codes'=8] {'codes'}, use_global_device_ids=true, to_apply=%region_16.20 | all-reduce | flops 2048 | bytes 16384 | tf_op jit(solution)/shard_map/psum | solution.py:76
  361.2 23.1 %while.130 = (s32[]{:T(128)}, f32[64,128]{1,0:T(8,128)S(1)}, s32[16,16]{1,0:T(8,128)}, bf16[64,128,128]{2,1,0:T(8,128)(2,1)}, bf16[16,128,128]{2,1,0:T(8,128)(2,...) while((s32[]{:T(128)}, f32[64,128]{1,0:T(8,128)S(1)}, ...), condition=%wide.region_18.22_spmd.clone, body=%wide.region_17.21_spmd.clone.sunk | while | flops 564178048 | bytes 15500781 | solution.py:92
  379.1 4.9 fusion.299
  384.4 56.3 %psum.61 = f32[8192]{0:T(1024)S(1)} all-reduce(f32[8192]{0:T(1024)S(1)} %bitcast.355), channel_id=1, replica_groups=mesh['frames'=16,'codes'=8] {'frames'}, use_global_device_ids=true, to_apply=%region_19.23 | all-reduce | flops 8192 | bytes 65536 | tf_op jit(solution)/shard_map/psum | solution.py:95
  440.7 24.2 %while.126 = (s32[]{:T(128)}, f32[16,128]{1,0:T(8,128)S(1)}, s32[16,16]{1,0:T(8,128)}, bf16[64,128,128]{2,1,0:T(8,128)(2,1)}, bf16[16,128,128]{2,1,0:T(8,128)(2,...) while((s32[]{:T(128)}, f32[16,128]{1,0:T(8,128)S(1)}, ...), condition=%wide.region_21.25_spmd, body=%wide.region_20.24_spmd.sunk | while | flops 551586560 | bytes 15473243 | solution.py:73
  447.8 5.0 fusion.276
  459.8 5.0 fusion.276
  464.9 26.1 %psum.62 = f32[16,128]{1,0:T(8,128)S(1)} all-reduce(f32[16,128]{1,0:T(8,128)S(1)} %get-tuple-element.1470), channel_id=1, replica_groups=mesh['frames'=16,'codes'=8] {'codes'}, use_global_device_ids=true, to_apply=%region_22.26 | all-reduce | flops 2048 | bytes 16384 | tf_op jit(solution)/shard_map/psum | solution.py:76
  491.0 23.1 %while.131 = (s32[]{:T(128)}, f32[64,128]{1,0:T(8,128)S(1)}, s32[16,16]{1,0:T(8,128)}, bf16[64,128,128]{2,1,0:T(8,128)(2,1)}, bf16[16,128,128]{2,1,0:T(8,128)(2,...) while((s32[]{:T(128)}, f32[64,128]{1,0:T(8,128)S(1)}, ...), condition=%wide.region_24.28_spmd.clone, body=%wide.region_23.27_spmd.clone.sunk | while | flops 564178048 | bytes 15500781 | solution.py:92
  514.1 56.3 %psum.63 = f32[8192]{0:T(1024)S(1)} all-reduce(f32[8192]{0:T(1024)S(1)} %bitcast.354), channel_id=1, replica_groups=mesh['frames'=16,'codes'=8] {'frames'}, use_global_device_ids=true, to_apply=%region_25.29 | all-reduce | flops 8192 | bytes 65536 | tf_op jit(solution)/shard_map/psum | solution.py:95
  570.5 28.2 %while.127 = (s32[]{:T(128)}, f32[2048,128]{1,0:T(8,128)S(1)}, s32[16,16]{1,0:T(8,128)}, bf16[64,128,128]{2,1,0:T(8,128)(2,1)}, bf16[16,128,128]{2,1,0:T(8,128)(...) while((s32[]{:T(128)}, f32[2048,128]{1,0:T(8,128)S(1)}, ...), condition=%wide.region_27.31_spmd, body=%wide.region_26.30_spmd.sunk | while | flops 1088588544 | bytes 21405224 | solution.py:115
  577.5 7.1 %fusion.279 = f32[8,128,128]{2,1,0:T(8,128)S(1)} fusion(bf16[8,16,128,128]{3,2,1,0:T(8,128)(2,1)} %bitcast.325, pred[8,16]{1,0:T(8,128)(4,1)S(1)} %get-tuple-element.2271, f32[8,16,128]{2,1,0:T(8,128)S(1)} %get-tuple-element.2272, f32[8,16]{1,0:T(8,128)S(1)} %constant_dynamic-slice_fusion.31, f32[8,16,128]{2,1,0:T(8,128)S(1)} %get-tuple-element.2273, ...), kind=kOutput, calls=%fused_computation.110.clone.1 | convolution fusion | flops 1088552960 | bytes 9320452 | tf_op jit(solution)/shard_map/while/body/eval_jaxpr/rsfk,rske->rfe/dot_general | solution.py:109
  591.6 7.1 %fusion.279 = f32[8,128,128]{2,1,0:T(8,128)S(1)} fusion(bf16[8,16,128,128]{3,2,1,0:T(8,128)(2,1)} %bitcast.325, pred[8,16]{1,0:T(8,128)(4,1)S(1)} %get-tuple-element.2271, f32[8,16,128]{2,1,0:T(8,128)S(1)} %get-tuple-element.2272, f32[8,16]{1,0:T(8,128)S(1)} %constant_dynamic-slice_fusion.31, f32[8,16,128]{2,1,0:T(8,128)S(1)} %get-tuple-element.2273, ...), kind=kOutput, calls=%fused_computation.110.clone.1 | convolution fusion | flops 1088552960 | bytes 9320452 | tf_op jit(solution)/shard_map/while/body/eval_jaxpr/rsfk,rske->rfe/dot_general | solution.py:109
  600.4 35.2 %reduce-scatter.2.cloned.1.call-done = f32[256,128]{1,0:T(8,128)} async-done(((f32[2048,128]{1,0:T(8,128)}), f32[256,128]{1,0:T(8,128)}) %reduce-scatter.2.cloned.1.call-update) | async-done | bytes 131088 | tf_op jit(solution)/shard_map/reduce_scatter | solution.py:114
  (272 shorter events, 154.4 us)
Async XLA Ops:
  7.2 50.4 %all-gather.2.cloned.1.call-start = ((), (), s32[]{:S(2)}) async-start(), calls=%async_computation.1 | async-start | bytes 2228224 | tf_op jit(solution)/shard_map/all_gather | solution.py:20
  7.9 627.7 %reduce-scatter.2.cloned.1.call-start = ((), (), s32[]{:S(2)}) async-start(), calls=%async_computation.2 | async-start | bytes 1179648 | tf_op jit(solution)/shard_map/reduce_scatter | solution.py:114
  62.8 4.7 copy-start.3
  74.8 4.7 copy-start.3
  99.9 4.7 copy-start.4
  111.4 4.7 copy-start.4
  181.8 4.7 copy-start.5
  193.9 4.7 copy-start.5
  233.3 4.7 copy-start.6
  244.8 4.7 copy-start.6
  311.1 50.1 %copy-start.2 = (f32[64,128]{1,0:T(8,128)S(1)}, f32[64,128]{1,0:T(8,128)}, u32[]{:S(2)}) copy-start(f32[64,128]{1,0:T(8,128)} %custom-call.2) | copy-start | bytes 98308
  313.5 4.7 copy-start.7
  325.6 4.7 copy-start.7
  362.8 4.7 copy-start.8
  374.4 4.7 copy-start.8
  440.7 50.3 %copy-start.1 = (f32[64,128]{1,0:T(8,128)S(1)}, f32[64,128]{1,0:T(8,128)}, u32[]{:S(2)}) copy-start(f32[64,128]{1,0:T(8,128)} %custom-call.3) | copy-start | bytes 98308
  443.1 4.7 copy-start.9
  455.2 4.7 copy-start.9
  492.6 4.7 copy-start.10
  504.2 4.7 copy-start.10
  572.8 4.7 copy-start.11
  586.9 4.7 copy-start.11
  598.8 1.0 copy-start
Sparse Core Ops, SparseCore 0:
  10.1 47.4 all-gather.1
  599.9 35.6 reduce-scatter.1
where the time goes:
time: 646 us; the launch traced here: 642 us
  blocking collectives  321 us (50%)
  local copies, waits for them, and re-layouts  106 us (16%)
  matrix products  96.5 us (15%)
  waiting for transfers between devices  83.3 us (13%)
  other arithmetic  20.1 us (3%)
  between operations  14.3 us (2%)
    psum x4, blocking collectives, per_device(): totals = lax.psum(partial_cols, 'frames')  227 us
    psum x4, blocking collectives, per_device(): u_tiles = 1.0 / lax.psum(partial_rows, 'codes')  93.7 us
    gather x18, local copies, waits for them, and re-layouts, kernel_block(): picked = jnp.take(book_tiles, index_block, axis=0)  84.1 us
    all_gather x1, waiting for transfers between devices, per_device(): codebook_all = lax.all_gather(codebook, 'frames', axis=0, tiled=True)  47.5 us
    dot_general x8, matrix products, row_visit(): jnp.einsum('rsfk,rsk->rf', kernel_half, chosen, preferred_element_type=jn...  40.1 us
    dot_general x8, matrix products, col_visit(): jnp.einsum('rsfk,rf->rsk', kernel_half, u_block, preferred_element_type=j...  39.6 us
    reduce_scatter x1, waiting for transfers between devices, per_device(): lax.psum_scatter(lax.fori_loop(0, span // local_group, mix_visit, jnp.zer...  35.2 us
    dot_general x2, matrix products, mix_visit(): jnp.einsum('rsfk,rske->rfe', weights, picked, preferred_element_type=jnp....  14.3 us
  transfers between devices with their start and end apart: 2, of which 2 were waited for; matrix products, arithmetic and copies ran while one was open for 0% of the time, Pallas kernels for 0%

commit v1 on v0

v1 whole, which is shorter than its diff:
```python
import functools
import math

import jax
import jax.numpy as jnp
from jax import lax
from jax.experimental import pallas as pl
from jax.experimental.pallas import tpu as pltpu
from jax.sharding import PartitionSpec as P

ITERS = 4
EPS = 1e-06
INV_TEMP = 10.0
TILE = 128
SLOTS = 16
ROWS = 16
NF = 16
NC = 8
OWN = 4
PAD = 8
F32 = jnp.float32
BF16 = jnp.bfloat16
NT = (((1,), (1,)), ((), ()))
MESH = pl.DeviceIdType.MESH
FAR = sorted(
    ((a, b) for a in range(4) for b in range(4) if (a, b) != (0, 0)),
    key=lambda d: -min(d[0], 4 - d[0]) - min(d[1], 4 - d[1]))


def tile_rows(i):
    return pl.ds(pl.multiple_of(i * TILE, TILE), TILE)


def share(p):
    return pl.ds(pl.multiple_of(p * PAD, PAD), PAD)


def column(row):
    return jnp.broadcast_to(row, (TILE, TILE)).T


def kernel(target, feat_hbm, code_hbm, cnt_s, cols_s, cols_hbm, q_out, log_out,
           feat, cols_v, book, K, fs, cs, pick, place, contrib, rowrx, colb, colf, v_ref, u_ref,
           tosib, fromsib, mine, yrx,
           feat_sem, cols_sem, code_sem, book_s, book_r, cs_s, cs_r, row_s, row_r, col_s, col_r,
           sib_s, sib_r, y_s, y_r):
    me_f = lax.axis_index("frames")
    me_c = lax.axis_index("codes")
    x, z = me_f // 4, lax.rem(me_f, 4)
    y, core = me_c // 2, lax.rem(me_c, 2)
    sub16 = lax.broadcasted_iota(jnp.int32, (ROWS, TILE), 0)
    lane16 = lax.broadcasted_iota(jnp.int32, (ROWS, TILE), 1)

    def peer_f(k):
        return lax.rem(me_f + k, NF)

    def peer_c(k):
        return lax.rem(me_c + k, NC)

    def send(src, dst, ss, rs, where):
        pltpu.make_async_remote_copy(
            src_ref=src, dst_ref=dst, send_sem=ss, recv_sem=rs,
            device_id=where, device_id_type=MESH,
        ).start()

    def drain(ref, sem):
        pltpu.make_async_copy(ref, ref, sem).wait()

    own_book = book.at[pl.ds(me_f * OWN, OWN)]
    code_copy = pltpu.make_async_copy(code_hbm, own_book, code_sem)
    code_copy.start()
    feat_copy = pltpu.make_async_copy(feat_hbm, feat, feat_sem)
    feat_copy.start()
    cols_copy = pltpu.make_async_copy(cols_hbm, cols_v, cols_sem)
    cols_copy.start()

    barrier = pltpu.get_barrier_semaphore()
    for k in range(1, NF):
        pl.semaphore_signal(barrier, inc=1, device_id={"frames": peer_f(k)}, device_id_type=MESH)
    for k in range(1, NC):
        pl.semaphore_signal(barrier, inc=1, device_id={"codes": peer_c(k)}, device_id_type=MESH)
    pl.semaphore_wait(barrier, NF - 1 + NC - 1)
    code_copy.wait()

    def at(h, first, second):
        dx, dz = (first, second) if h == 0 else (second, first)
        return lax.rem(x + dx, 4) * 4 + lax.rem(z + dz, 4)

    def chunk(h, first, second, q=None):
        base = at(h, first, second) * OWN + 2 * h
        return book.at[pl.ds(base, 2)] if q is None else book.at[pl.ds(base + q, 1)]

    def pass_on(h, stage, way, ref, first, second):
        send(ref, ref, book_s, book_r.at[h, stage, way], {"frames": at(h, first, second)})

    def first_sends(h):
        pass_on(h, 0, 0, chunk(h, 0, 0), 1, 0)
        pass_on(h, 0, 1, chunk(h, 0, 0), 3, 0)

    def first_forwards(h):
        drain(chunk(h, 3, 0), book_r.at[h, 0, 0])
        pass_on(h, 1, 0, chunk(h, 3, 0, 0), 1, 0)
        drain(chunk(h, 1, 0), book_r.at[h, 0, 1])
        pass_on(h, 1, 1, chunk(h, 1, 0, 1), 3, 0)

    def second_sends(h, j):
        pass_on(h, 2 + j, 0, chunk(h, j, 0), 0, 1)
        pass_on(h, 2 + j, 1, chunk(h, j, 0), 0, 3)

    def second_forwards(h, j):
        drain(chunk(h, j, 3), book_r.at[h, 2 + j, 0])
        pass_on(h, 6 + j, 0, chunk(h, j, 3, 0), 0, 1)
        drain(chunk(h, j, 1), book_r.at[h, 2 + j, 1])
        pass_on(h, 6 + j, 1, chunk(h, j, 1, 1), 0, 3)

    for h in range(2):
        first_sends(h)
    for h in range(2):
        second_sends(h, 0)

    scales = []
    for t in range(OWN):
        own = book[me_f * OWN + t].astype(F32)
        scales.append(lax.rsqrt(jnp.sum((own * own).T, axis=0, keepdims=True) / TILE + EPS))
    cs[share(me_f), :] = jnp.concatenate(scales + [jnp.ones((PAD - OWN, TILE), F32)], axis=0)
    for k in range(1, NF):
        send(cs.at[share(me_f)], cs.at[share(me_f)], cs_s, cs_r, {"frames": peer_f(k)})

    for h in range(2):
        first_forwards(h)
    for h in range(2):
        second_sends(h, 1)
        second_sends(h, 3)
    for h in range(2):
        second_forwards(h, 0)
    for h in range(2):
        drain(chunk(h, 2, 0, 0), book_r.at[h, 1, 0])
        drain(chunk(h, 2, 0, 1), book_r.at[h, 1, 1])
        second_sends(h, 2)

    feat_copy.wait()
    cols_copy.wait()

    def frame_scale(i, _):
        part = feat[tile_rows(i), :].astype(F32)
        m = jnp.sum(part * part, axis=1, keepdims=True) / TILE
        s = lax.rsqrt(m + EPS) * (INV_TEMP / TILE * math.log2(math.e))
        fs[tile_rows(i), :] = jnp.broadcast_to(s, (TILE, TILE))
        return 0

    lax.fori_loop(0, ROWS, frame_scale, 0)
    for h in range(2):
        second_forwards(h, 1)
        second_forwards(h, 3)

    count = jnp.zeros((ROWS, SLOTS), jnp.int32)
    for i in range(ROWS):
        count = jnp.where(lax.broadcasted_iota(jnp.int32, count.shape, 0) == i, cnt_s[0, i], count)
    cv = jnp.where(lax.broadcasted_iota(jnp.int32, count.shape, 1) < count, cols_v[:, 0, :], -1)
    for s in range(SLOTS):
        hot = (jnp.broadcast_to(cv[:, s:s + 1], (ROWS, TILE)) == lane16).astype(F32)
        pick[s * ROWS:(s + 1) * ROWS, :] = hot[:, :NF * OWN].astype(BF16)
        contrib[s * ROWS:(s + 1) * ROWS, :] = hot
    for h in range(2):
        turned = contrib[h * TILE:(h + 1) * TILE, :].T[:NF * OWN].astype(BF16)
        for j in range(3):
            place[:, j * 2 * TILE + h * TILE:j * 2 * TILE + (h + 1) * TILE] = turned

    for h in range(2):
        second_forwards(h, 2)
    for h in range(2):
        for j in range(4):
            drain(chunk(h, j, 2, 0), book_r.at[h, 6 + j, 0])
            drain(chunk(h, j, 2, 1), book_r.at[h, 6 + j, 1])
    drain(cs.at[pl.ds(0, (NF - 1) * PAD)], cs_r)

    def build(i, _):
        a = feat[tile_rows(i), :]
        f = fs[tile_rows(i), :]
        f = jnp.concatenate([f, f], axis=1)
        for s in range(0, SLOTS, 2):
            at2 = [cols_s[i, 0, s + j] for j in range(2)]
            words = jnp.concatenate([book[c] for c in at2], axis=0)
            scale = jnp.concatenate(
                [cs[pl.ds((c // OWN) * PAD + lax.rem(c, OWN), 1), :] for c in at2], axis=1)
            p = lax.dot_general(a, words, NT, preferred_element_type=F32)
            K[tile_rows(i), s * TILE:(s + 2) * TILE] = jnp.exp2(p * f * scale).astype(BF16)
        return 0

    lax.fori_loop(0, ROWS, build, 0, unroll=2)

    v_ref[...] = jnp.ones_like(v_ref)

    def sweep(it, last):
        chosen = jnp.dot(pick[...], v_ref[...].astype(BF16), preferred_element_type=F32).astype(BF16)
        V = jnp.concatenate([chosen[s * ROWS:(s + 1) * ROWS, :] for s in range(SLOTS)], axis=1)

        r = lax.dot_general(V, K[...], NT, preferred_element_type=F32)
        sums = r[:, :TILE]
        for i in range(1, ROWS):
            sums = jnp.where(sub16 == i, r[:, i * TILE:(i + 1) * TILE], sums)
        rowrx[it, me_c] = sums
        for dy, dk in ((2, 1), (2, 0), (1, 1), (3, 1), (1, 0), (3, 0), (0, 1)):
            send(rowrx.at[it, me_c], rowrx.at[it, me_c], row_s.at[it], row_r.at[it],
                 {"codes": lax.rem(y + dy, 4) * 2 + lax.rem(core + dk, 2)})
        drain(rowrx.at[it, pl.ds(0, NC - 1)], row_r.at[it])
        total = rowrx[it, 0]
        for c in range(1, NC):
            total = total + rowrx[it, c]
        u = 1.0 / total
        u_ref[...] = u
        U = jnp.concatenate([jnp.where(sub16 == i, u, 0.0) for i in range(ROWS)], axis=1).astype(BF16)

        r = jnp.dot(U, K[...], preferred_element_type=F32)
        rest = jnp.concatenate([r[:, s * TILE:(s + 1) * TILE] for s in range(SLOTS)], axis=0)
        hi = rest.astype(BF16)
        rest = rest - hi.astype(F32)
        mid = rest.astype(BF16)
        lo = (rest - mid.astype(F32)).astype(BF16)
        cols = jnp.dot(place[...], jnp.concatenate([hi, mid, lo], axis=0), preferred_element_type=F32)
        got = colf if last else colb.at[it]
        got[me_f] = cols.astype(got.dtype)
        for dx, dz in FAR:
            send(got.at[me_f], got.at[me_f], col_s.at[it], col_r.at[it], {"frames": at(0, dx, dz)})
        drain(got.at[pl.ds(0, NF - 1)], col_r.at[it])
        csum = got[0].astype(F32)
        for p in range(1, NF):
            csum = csum + got[p].astype(F32)
        v_ref[...] = target / csum

    def early(it, _):
        sweep(it, False)
        return 0

    lax.fori_loop(0, ITERS - 1, early, 0)
    sweep(ITERS - 1, True)
    log_out[...] = jnp.log(jnp.concatenate(
        [v_ref[pl.ds(me_f * OWN + t, 1), :] for t in range(OWN)], axis=0))

    def mix(c, dst):
        def one(j, _):
            i = 2 * c + j
            n = cnt_s[0, i]
            weights, words = [], []
            for s in range(SLOTS):
                word = cols_s[i, 0, s]
                scale = v_ref[pl.ds(word, 1), :] * jnp.where(s < n, 1.0, 0.0)
                k = K[tile_rows(i), s * TILE:(s + 1) * TILE].astype(F32)
                weights.append((k * scale).astype(BF16))
                words.append(book[word])
            dst[tile_rows(j), :] = jnp.dot(
                jnp.concatenate(weights, axis=1), jnp.concatenate(words, axis=0),
                preferred_element_type=F32)
            return 0

        lax.fori_loop(0, 2, one, 0)

    def chip(k):
        return lax.rem(y + 2 + k * (k + 1) // 2, 4)

    def join(k):
        drain(fromsib.at[k], sib_r.at[k])
        mine[k] = mine[k] + fromsib[k]

    def forward(k):
        join(k)
        send(mine.at[k], yrx.at[k], y_s.at[k], y_r.at[k], {"codes": chip(k) * 2 + core})

    def mix_step(k, _):
        mix(chip(k) * 2 + 1 - core, tosib.at[k])
        send(tosib.at[k], fromsib.at[k], sib_s.at[k], sib_r.at[k], {"codes": y * 2 + 1 - core})
        mix(chip(k) * 2 + core, mine.at[k])

        @pl.when(k > 0)
        def _():
            forward(k - 1)

        return 0

    lax.fori_loop(0, 4, mix_step, 0)
    join(3)
    for k in range(3):
        drain(yrx.at[k], y_r.at[k])
    for j in range(2):
        rows = slice(j * TILE, (j + 1) * TILE)
        acc = mine[3, rows, :]
        for k in range(3):
            acc = acc + yrx[k, rows, :]
        q_out[rows, :] = acc * column(u_ref[pl.ds(2 * me_c + j, 1), :])

    drain(book.at[pl.ds(0, 60)], book_s)
    drain(cs.at[pl.ds(0, (NF - 1) * PAD)], cs_s)
    for it in range(ITERS):
        drain(rowrx.at[it, pl.ds(0, NC - 1)], row_s.at[it])
        got = colf if it == ITERS - 1 else colb.at[it]
        drain(got.at[pl.ds(0, NF - 1)], col_s.at[it])
    for k in range(4):
        drain(tosib.at[k], sib_s.at[k])
    for k in range(3):
        drain(mine.at[k], y_s.at[k])


def per_device(target, features, codebook, tile_count, tile_cols):
    vmem = pl.BlockSpec(memory_space=pltpu.VMEM)
    smem = pl.BlockSpec(memory_space=pltpu.SMEM)
    hbm = pl.BlockSpec(memory_space=pl.ANY)
    dma = pltpu.SemaphoreType.DMA
    quantized, logs = pl.pallas_call(
        functools.partial(kernel, target),
        out_shape=(
            jax.ShapeDtypeStruct((2 * TILE, TILE), F32),
            jax.ShapeDtypeStruct((OWN, TILE), F32),
        ),
        in_specs=[hbm, hbm, smem, smem, hbm],
        out_specs=(vmem, vmem),
        scratch_shapes=[
            pltpu.VMEM((ROWS * TILE, TILE), BF16),
            pltpu.VMEM((ROWS, 1, SLOTS), jnp.int32),
            pltpu.VMEM((NF * OWN, TILE, TILE), BF16),
            pltpu.VMEM((ROWS * TILE, SLOTS * TILE), BF16),
            pltpu.VMEM((ROWS * TILE, TILE), F32),
            pltpu.VMEM((NF * PAD, TILE), F32),
            pltpu.VMEM((SLOTS * ROWS, NF * OWN), BF16),
            pltpu.VMEM((NF * OWN, 3 * SLOTS * ROWS), BF16),
            pltpu.VMEM((SLOTS * ROWS, TILE), F32),
            pltpu.VMEM((ITERS, NC, ROWS, TILE), F32),
            pltpu.VMEM((ITERS - 1, NF, NF * OWN, TILE), BF16),
            pltpu.VMEM((NF, NF * OWN, TILE), F32),
            pltpu.VMEM((NF * OWN, TILE), F32),
            pltpu.VMEM((ROWS, TILE), F32),
            pltpu.VMEM((4, 2 * TILE, TILE), F32),
            pltpu.VMEM((4, 2 * TILE, TILE), F32),
            pltpu.VMEM((4, 2 * TILE, TILE), F32),
            pltpu.VMEM((3, 2 * TILE, TILE), F32),
            dma, dma, dma, dma, dma((2, 10, 2)), dma, dma,
            dma((ITERS,)), dma((ITERS,)), dma((ITERS,)), dma((ITERS,)),
            dma((4,)), dma((4,)), dma((4,)), dma((4,)),
        ],
        compiler_params=pltpu.CompilerParams(
            collective_id=0, has_side_effects=True, vmem_limit_bytes=60 * 2**20),
    )(features, codebook.reshape(OWN, TILE, TILE), tile_count.reshape(1, ROWS), tile_cols, tile_cols)
    return quantized, logs.reshape(OWN * TILE)


def solution(mesh):
    target = 32768 / 65536
    return jax.shard_map(
        functools.partial(per_device, target),
        mesh=mesh,
        in_specs=(
            P("frames", None),
            P(("codes", "frames"), None),
            P("frames", "codes"),
            P("frames", "codes", None),
        ),
        out_specs=(P(("frames", "codes"), None), P(("codes", "frames"))),
        check_vma=False,
    )
```

time: 646 us -> 97.3 us (0.15)
  blocking collectives: 321 us -> 0 us
  local copies, waits for them, and re-layouts: 106 us -> 2.15 us
  matrix products: 96.5 us -> 0 us
  Pallas kernels: 0 us -> 94.3 us
  waiting for transfers between devices: 83.3 us -> 0 us
  other arithmetic: 20.1 us -> 0 us
  between operations: 14.3 us -> 0.65 us
    psum x8 -> x0, blocking collectives: 321 us -> none  [the longest x4 227 us: per_device(): totals = lax.psum(partial_cols, 'frames')]
    gather x46 -> x0, local copies, waits for them, and re-layouts: 103 us -> none  [the longest x18 84.1 us: kernel_block(): picked = jnp.take(book_tiles, index_block, axis=0)]
    dot_general x26 -> x0, matrix products: 96.5 us -> none  [the longest x8 40.1 us: row_visit(): jnp.einsum('rsfk,rsk->rf', kernel_half, chosen, preferred_element_type=jn...]
    pallas_call x0 -> x1, Pallas kernels: none -> 94.3 us  [per_device(): pl.pallas_call(functools.partial(kernel, target), out_shape=(jax.ShapeDty...]
    all_gather x1 -> x0, waiting for transfers between devices: 47.5 us -> none  [per_device(): codebook_all = lax.all_gather(codebook, 'frames', axis=0, tiled=True)]
    reduce_scatter x1 -> x0, waiting for transfers between devices: 35.2 us -> none  [per_device(): lax.psum_scatter(lax.fori_loop(0, span // local_group, mix_visit, jnp.zer...]
    and x18 -> x0, other arithmetic: 12.6 us -> none  [kernel_block(): picked = jnp.take(book_tiles, index_block, axis=0)]
  transfers between devices with their start and end apart: 2 -> 0, of which waited for: 2 -> 0; matrix products, arithmetic and copies ran while one was open for 0% -> 0% of each run, Pallas kernels for 0% -> 0%
where the time goes in v1:
time: 97.3 us; the launch traced here: 97.1 us
  Pallas kernels  94.3 us (97%)
  local copies, waits for them, and re-layouts  2.15 us (2%)
    pallas_call x1, Pallas kernels, per_device(): pl.pallas_call(functools.partial(kernel, target), out_shape=(jax.ShapeDty...  94.3 us
    unnamed x4, local copies, waits for them, and re-layouts  2.15 us

profile of v1, /device:TPU:1, one launch (start us, length us, event | category | flops | bytes accessed | tf_op | source)
XLA Modules:
  0.0 97.1 jit_solution(14110727104536987063)
XLA Ops:
  0.6 94.3 %shard_map.59 = (f32[256,128]{1,0:T(8,128)}, f32[4,128]{1,0:T(4,128)}) custom-call(bf16[2048,128]{1,0:T(8,128)(2,1)} %feat_hbm.1, bf16[4,128,128]{2,1,0:T(8,128)(2,1)} %bitcast.3, s32[1,16]{1,0:T(1,128)} %bitcast.5, s32[16,1,16]{2,1,0:T(1,128)} %cols_hbm.1, s32[16,1,16]{2,1,0:T(1,128)} %cols_hbm.1), custom_call_target="tpu_custom_call" | custom-call | tf_op jit(solution)/shard_map/pallas_call | solution.py:308
  94.9 0.0 copy-start
  94.9 1.6 %copy.8 = f32[256,128]{1,0:T(8,128)} copy(f32[256,128]{1,0:T(8,128)} %get-tuple-element.8) | data formatting | bytes 262144
  96.5 0.0 copy-done
  96.5 0.6 copy.9
Async XLA Ops:
  94.9 1.6 %copy-start = (f32[4,128]{1,0:T(4,128)S(1)}, f32[4,128]{1,0:T(4,128)}, u32[]{:S(2)}) copy-start(f32[4,128]{1,0:T(4,128)} %get-tuple-element.5) | copy-start | bytes 6148

commit v2 on v1

--- a/solution.py
+++ b/solution.py
@@ -16,15 +16,14 @@
 ROWS = 16
 NF = 16
 NC = 8
+SPLIT = 5
+HALF = 32
 OWN = 4
 PAD = 8
 F32 = jnp.float32
 BF16 = jnp.bfloat16
 NT = (((1,), (1,)), ((), ()))
 MESH = pl.DeviceIdType.MESH
-FAR = sorted(
-    ((a, b) for a in range(4) for b in range(4) if (a, b) != (0, 0)),
-    key=lambda d: -min(d[0], 4 - d[0]) - min(d[1], 4 - d[1]))
 
 
 def tile_rows(i):
@@ -40,7 +39,7 @@
 
 
 def kernel(target, feat_hbm, code_hbm, cnt_s, cols_s, cols_hbm, q_out, log_out,
-           feat, cols_v, book, K, fs, cs, pick, place, contrib, rowrx, colb, colf, v_ref, u_ref,
+           feat, cols_v, book, K, exact, fs, cs, pick, place, contrib, rowrx, sums, v_ref, u_ref,
            tosib, fromsib, mine, yrx,
            feat_sem, cols_sem, code_sem, book_s, book_r, cs_s, cs_r, row_s, row_r, col_s, col_r,
            sib_s, sib_r, y_s, y_r):
@@ -49,6 +48,8 @@
     x, z = me_f // 4, lax.rem(me_f, 4)
     y, core = me_c // 2, lax.rem(me_c, 2)
     sub16 = lax.broadcasted_iota(jnp.int32, (ROWS, TILE), 0)
+    lane = lax.broadcasted_iota(jnp.int32, (TILE, TILE), 1)
+    sub8 = lax.broadcasted_iota(jnp.int32, (8, TILE), 0)
     lane16 = lax.broadcasted_iota(jnp.int32, (ROWS, TILE), 1)
 
     def peer_f(k):
@@ -184,56 +185,77 @@
             scale = jnp.concatenate(
                 [cs[pl.ds((c // OWN) * PAD + lax.rem(c, OWN), 1), :] for c in at2], axis=1)
             p = lax.dot_general(a, words, NT, preferred_element_type=F32)
-            K[tile_rows(i), s * TILE:(s + 2) * TILE] = jnp.exp2(p * f * scale).astype(BF16)
+            k = jnp.exp2(p * f * scale)
+            exact[tile_rows(i), s * TILE:(s + 2) * TILE] = k
+            K[tile_rows(i), s * TILE:(s + 2) * TILE] = k.astype(BF16)
         return 0
 
     lax.fori_loop(0, ROWS, build, 0, unroll=2)
 
     v_ref[...] = jnp.ones_like(v_ref)
 
-    def sweep(it, last):
-        chosen = jnp.dot(pick[...], v_ref[...].astype(BF16), preferred_element_type=F32).astype(BF16)
-        V = jnp.concatenate([chosen[s * ROWS:(s + 1) * ROWS, :] for s in range(SLOTS)], axis=1)
-
-        r = lax.dot_general(V, K[...], NT, preferred_element_type=F32)
-        sums = r[:, :TILE]
-        for i in range(1, ROWS):
-            sums = jnp.where(sub16 == i, r[:, i * TILE:(i + 1) * TILE], sums)
-        rowrx[it, me_c] = sums
-        for dy, dk in ((2, 1), (2, 0), (1, 1), (3, 1), (1, 0), (3, 0), (0, 1)):
-            send(rowrx.at[it, me_c], rowrx.at[it, me_c], row_s.at[it], row_r.at[it],
-                 {"codes": lax.rem(y + dy, 4) * 2 + lax.rem(core + dk, 2)})
-        drain(rowrx.at[it, pl.ds(0, NC - 1)], row_r.at[it])
-        total = rowrx[it, 0]
-        for c in range(1, NC):
-            total = total + rowrx[it, c]
-        u = 1.0 / total
-        u_ref[...] = u
-        U = jnp.concatenate([jnp.where(sub16 == i, u, 0.0) for i in range(ROWS)], axis=1).astype(BF16)
-
-        r = jnp.dot(U, K[...], preferred_element_type=F32)
-        rest = jnp.concatenate([r[:, s * TILE:(s + 1) * TILE] for s in range(SLOTS)], axis=0)
+    def hop(it, stage, h, values):
+        along_x = stage == h
+        slot = sums.at[it, stage, h, x if along_x else z]
+        slot[...] = values
+        for k in (2, 1, 3):
+            where = at(0, k, 0) if along_x else at(0, 0, k)
+            send(slot, slot, col_s.at[it, stage, h], col_r.at[it, stage, h], {"frames": where})
+
+    def gathered(it, stage, h):
+        drain(sums.at[it, stage, h, pl.ds(0, 3)], col_r.at[it, stage, h])
+        return (sums[it, stage, h, 0] + sums[it, stage, h, 1]) + (sums[it, stage, h, 2] + sums[it, stage, h, 3])
+
+    def sweep(it, _):
+        contrib[...] = jnp.dot(pick[...], v_ref[...].astype(BF16), preferred_element_type=F32)
+        V = jnp.concatenate(
+            [contrib[s * ROWS:(s + 1) * ROWS, :] for s in range(SPLIT)], axis=1).astype(BF16)
+
+        r = lax.dot_general(V, K[:, :SPLIT * TILE], NT, preferred_element_type=F32)
+        side = jnp.zeros((TILE, TILE), F32)
+        for g in range(2):
+            for i in range(g * 8, g * 8 + 8):
+                acc = jnp.zeros((TILE, TILE), F32)
+                for s in range(SPLIT, SLOTS):
+                    k = K[i * TILE:(i + 1) * TILE, s * TILE:(s + 1) * TILE].astype(F32)
+                    acc = acc + k * contrib[s * ROWS + i:s * ROWS + i + 1, :]
+                side = jnp.where(lane == i, jnp.sum(acc, axis=1, keepdims=True), side)
+            total = side.T[g * 8:g * 8 + 8]
+            for i in range(g * 8, g * 8 + 8):
+                total = total + jnp.where(
+                    sub8 == i - g * 8, r[g * 8:g * 8 + 8, i * TILE:(i + 1) * TILE], 0.0)
+            slot = rowrx.at[it, g, me_c]
+            slot[...] = total
+            for dy, dk in ((2, 1), (2, 0), (1, 1), (3, 1), (1, 0), (3, 0), (0, 1)):
+                send(slot, slot, row_s.at[it, g], row_r.at[it, g],
+                     {"codes": lax.rem(y + dy, 4) * 2 + lax.rem(core + dk, 2)})
+        parts = []
+        for g in range(2):
+            drain(rowrx.at[it, g, pl.ds(0, NC - 1)], row_r.at[it, g])
+            total = rowrx[it, g, 0]
+            for c in range(1, NC):
+                total = total + rowrx[it, g, c]
+            u = 1.0 / total
+            u_ref[g * 8:g * 8 + 8, :] = u
+            U = jnp.concatenate(
+                [jnp.where(sub8 == i, u, 0.0) for i in range(8)], axis=1).astype(BF16)
+            parts.append(jnp.dot(U, K[g * 8 * TILE:(g + 1) * 8 * TILE, :], preferred_element_type=F32))
+        rest = jnp.concatenate(
+            [parts[g][:, s * TILE:(s + 1) * TILE] for s in range(SLOTS) for g in range(2)], axis=0)
         hi = rest.astype(BF16)
         rest = rest - hi.astype(F32)
         mid = rest.astype(BF16)
         lo = (rest - mid.astype(F32)).astype(BF16)
         cols = jnp.dot(place[...], jnp.concatenate([hi, mid, lo], axis=0), preferred_element_type=F32)
-        got = colf if last else colb.at[it]
-        got[me_f] = cols.astype(got.dtype)
-        for dx, dz in FAR:
-            send(got.at[me_f], got.at[me_f], col_s.at[it], col_r.at[it], {"frames": at(0, dx, dz)})
-        drain(got.at[pl.ds(0, NF - 1)], col_r.at[it])
-        csum = got[0].astype(F32)
-        for p in range(1, NF):
-            csum = csum + got[p].astype(F32)
+        for h in range(2):
+            hop(it, 0, h, cols[h * HALF:(h + 1) * HALF])
+        for h in range(2):
+            hop(it, 1, h, gathered(it, 0, h))
+        csum = jnp.concatenate([gathered(it, 1, h) for h in range(2)], axis=0)
         v_ref[...] = target / csum
-
-    def early(it, _):
-        sweep(it, False)
         return 0
 
-    lax.fori_loop(0, ITERS - 1, early, 0)
-    sweep(ITERS - 1, True)
+    lax.fori_loop(0, ITERS, sweep, 0)
     log_out[...] = jnp.log(jnp.concatenate(
         [v_ref[pl.ds(me_f * OWN + t, 1), :] for t in range(OWN)], axis=0))
 
@@ -245,7 +267,7 @@
             for s in range(SLOTS):
                 word = cols_s[i, 0, s]
                 scale = v_ref[pl.ds(word, 1), :] * jnp.where(s < n, 1.0, 0.0)
-                k = K[tile_rows(i), s * TILE:(s + 1) * TILE].astype(F32)
+                k = exact[tile_rows(i), s * TILE:(s + 1) * TILE]
                 weights.append((k * scale).astype(BF16))
                 words.append(book[word])
             dst[tile_rows(j), :] = jnp.dot(
@@ -291,9 +313,11 @@
     drain(book.at[pl.ds(0, 60)], book_s)
     drain(cs.at[pl.ds(0, (NF - 1) * PAD)], cs_s)
     for it in range(ITERS):
-        drain(rowrx.at[it, pl.ds(0, NC - 1)], row_s.at[it])
-        got = colf if it == ITERS - 1 else colb.at[it]
-        drain(got.at[pl.ds(0, NF - 1)], col_s.at[it])
+        for g in range(2):
+            drain(rowrx.at[it, g, pl.ds(0, NC - 1)], row_s.at[it, g])
+        for stage in range(2):
+            for h in range(2):
+                drain(sums.at[it, stage, h, pl.ds(0, 3)], col_s.at[it, stage, h])
     for k in range(4):
         drain(tosib.at[k], sib_s.at[k])
     for k in range(3):
@@ -318,14 +342,14 @@
             pltpu.VMEM((ROWS, 1, SLOTS), jnp.int32),
             pltpu.VMEM((NF * OWN, TILE, TILE), BF16),
             pltpu.VMEM((ROWS * TILE, SLOTS * TILE), BF16),
+            pltpu.VMEM((ROWS * TILE, SLOTS * TILE), F32),
             pltpu.VMEM((ROWS * TILE, TILE), F32),
             pltpu.VMEM((NF * PAD, TILE), F32),
             pltpu.VMEM((SLOTS * ROWS, NF * OWN), BF16),
             pltpu.VMEM((NF * OWN, 3 * SLOTS * ROWS), BF16),
             pltpu.VMEM((SLOTS * ROWS, TILE), F32),
-            pltpu.VMEM((ITERS, NC, ROWS, TILE), F32),
-            pltpu.VMEM((ITERS - 1, NF, NF * OWN, TILE), BF16),
-            pltpu.VMEM((NF, NF * OWN, TILE), F32),
+            pltpu.VMEM((ITERS, 2, NC, 8, TILE), F32),
+            pltpu.VMEM((ITERS, 2, 2, 4, HALF, TILE), F32),
             pltpu.VMEM((NF * OWN, TILE), F32),
             pltpu.VMEM((ROWS, TILE), F32),
             pltpu.VMEM((4, 2 * TILE, TILE), F32),
@@ -333,7 +357,7 @@
             pltpu.VMEM((4, 2 * TILE, TILE), F32),
             pltpu.VMEM((3, 2 * TILE, TILE), F32),
             dma, dma, dma, dma, dma((2, 10, 2)), dma, dma,
-            dma((ITERS,)), dma((ITERS,)), dma((ITERS,)), dma((ITERS,)),
+            dma((ITERS, 2)), dma((ITERS, 2)), dma((ITERS, 2, 2)), dma((ITERS, 2, 2)),
             dma((4,)), dma((4,)), dma((4,)), dma((4,)),
         ],
         compiler_params=pltpu.CompilerParams(

time: 97.3 us -> 95.2 us (0.978)
  Pallas kernels: 94.3 us -> 92.3 us
    pallas_call x1, Pallas kernels: 94.3 us -> 92.3 us  [per_device(): pl.pallas_call(functools.partial(kernel, target), out_shape=(jax.ShapeDty...]
where the time goes in v2:
time: 95.2 us; the launch traced here: 95.1 us
  Pallas kernels  92.3 us (97%)
  local copies, waits for them, and re-layouts  2.15 us (2%)
    pallas_call x1, Pallas kernels, per_device(): pl.pallas_call(functools.partial(kernel, target), out_shape=(jax.ShapeDty...  92.3 us
    unnamed x4, local copies, waits for them, and re-layouts  2.15 us

profile of v2, /device:TPU:1, one launch (start us, length us, event | category | flops | bytes accessed | tf_op | source)
XLA Modules:
  0.0 95.1 jit_solution(13848711979900078875)
XLA Ops:
  0.6 92.3 %shard_map.59 = (f32[256,128]{1,0:T(8,128)}, f32[4,128]{1,0:T(4,128)}) custom-call(bf16[2048,128]{1,0:T(8,128)(2,1)} %feat_hbm.1, bf16[4,128,128]{2,1,0:T(8,128)(2,1)} %bitcast.3, s32[1,16]{1,0:T(1,128)} %bitcast.5, s32[16,1,16]{2,1,0:T(1,128)} %cols_hbm.1, s32[16,1,16]{2,1,0:T(1,128)} %cols_hbm.1), custom_call_target="tpu_custom_call" | custom-call | tf_op jit(solution)/shard_map/pallas_call | solution.py:332
  92.9 0.0 copy-start
  92.9 1.6 %copy.8 = f32[256,128]{1,0:T(8,128)} copy(f32[256,128]{1,0:T(8,128)} %get-tuple-element.8) | data formatting | bytes 262144
  94.5 0.0 copy-done
  94.5 0.6 copy.9
Async XLA Ops:
  92.9 1.6 %copy-start = (f32[4,128]{1,0:T(4,128)S(1)}, f32[4,128]{1,0:T(4,128)}, u32[]{:S(2)}) copy-start(f32[4,128]{1,0:T(4,128)} %get-tuple-element.5) | copy-start | bytes 6148

commit v3 on v2

--- a/solution.py
+++ b/solution.py
@@ -18,6 +18,7 @@
 NC = 8
 SPLIT = 5
 HALF = 32
+DIRECT = (2,)
 OWN = 4
 PAD = 8
 F32 = jnp.float32
@@ -95,24 +96,30 @@
         send(ref, ref, book_s, book_r.at[h, stage, way], {"frames": at(h, first, second)})
 
     def first_sends(h):
-        pass_on(h, 0, 0, chunk(h, 0, 0), 1, 0)
-        pass_on(h, 0, 1, chunk(h, 0, 0), 3, 0)
+        pass_on(h, 0, 0, chunk(h, 0, 0, 0), 1, 0)
+        pass_on(h, 0, 1, chunk(h, 0, 0, 1), 3, 0)
+        pass_on(h, 10, 0, chunk(h, 0, 0, 1), 1, 0)
+        pass_on(h, 10, 1, chunk(h, 0, 0, 0), 3, 0)
 
     def first_forwards(h):
-        drain(chunk(h, 3, 0), book_r.at[h, 0, 0])
+        drain(chunk(h, 3, 0, 0), book_r.at[h, 0, 0])
         pass_on(h, 1, 0, chunk(h, 3, 0, 0), 1, 0)
-        drain(chunk(h, 1, 0), book_r.at[h, 0, 1])
+        drain(chunk(h, 1, 0, 1), book_r.at[h, 0, 1])
         pass_on(h, 1, 1, chunk(h, 1, 0, 1), 3, 0)
 
     def second_sends(h, j):
         pass_on(h, 2 + j, 0, chunk(h, j, 0), 0, 1)
         pass_on(h, 2 + j, 1, chunk(h, j, 0), 0, 3)
+        if j in DIRECT:
+            pass_on(h, 6 + j, 0, chunk(h, j, 0), 0, 2)
 
     def second_forwards(h, j):
         drain(chunk(h, j, 3), book_r.at[h, 2 + j, 0])
-        pass_on(h, 6 + j, 0, chunk(h, j, 3, 0), 0, 1)
+        if j not in DIRECT:
+            pass_on(h, 6 + j, 0, chunk(h, j, 3, 0), 0, 1)
         drain(chunk(h, j, 1), book_r.at[h, 2 + j, 1])
-        pass_on(h, 6 + j, 1, chunk(h, j, 1, 1), 0, 3)
+        if j not in DIRECT:
+            pass_on(h, 6 + j, 1, chunk(h, j, 1, 1), 0, 3)
 
     for h in range(2):
         first_sends(h)
@@ -130,8 +137,10 @@
     for h in range(2):
         first_forwards(h)
     for h in range(2):
+        drain(chunk(h, 3, 0, 1), book_r.at[h, 10, 0])
+        second_sends(h, 3)
+        drain(chunk(h, 1, 0, 0), book_r.at[h, 10, 1])
         second_sends(h, 1)
-        second_sends(h, 3)
     for h in range(2):
         second_forwards(h, 0)
     for h in range(2):
@@ -171,6 +180,9 @@
         second_forwards(h, 2)
     for h in range(2):
         for j in range(4):
+            if j in DIRECT:
+                drain(chunk(h, j, 2), book_r.at[h, 6 + j, 0])
+                continue
             drain(chunk(h, j, 2, 0), book_r.at[h, 6 + j, 0])
             drain(chunk(h, j, 2, 1), book_r.at[h, 6 + j, 1])
     drain(cs.at[pl.ds(0, (NF - 1) * PAD)], cs_r)
@@ -356,7 +368,7 @@
             pltpu.VMEM((4, 2 * TILE, TILE), F32),
             pltpu.VMEM((4, 2 * TILE, TILE), F32),
             pltpu.VMEM((3, 2 * TILE, TILE), F32),
-            dma, dma, dma, dma, dma((2, 10, 2)), dma, dma,
+            dma, dma, dma, dma, dma((2, 11, 2)), dma, dma,
             dma((ITERS, 2)), dma((ITERS, 2)), dma((ITERS, 2, 2)), dma((ITERS, 2, 2)),
             dma((4,)), dma((4,)), dma((4,)), dma((4,)),
         ],

time: 95.2 us -> 94.5 us (level)
  no operation moved by 1% of the time
where the time goes in v3:
time: 94.5 us; the launch traced here: 94.4 us
  Pallas kernels  91.6 us (97%)
  local copies, waits for them, and re-layouts  2.15 us (2%)
    pallas_call x1, Pallas kernels, per_device(): pl.pallas_call(functools.partial(kernel, target), out_shape=(jax.ShapeDty...  91.6 us
    unnamed x4, local copies, waits for them, and re-layouts  2.15 us

profile of v3, /device:TPU:1, one launch (start us, length us, event | category | flops | bytes accessed | tf_op | source)
XLA Modules:
  0.0 94.4 jit_solution(1971989908579157751)
XLA Ops:
  0.6 91.6 %shard_map.59 = (f32[256,128]{1,0:T(8,128)}, f32[4,128]{1,0:T(4,128)}) custom-call(bf16[2048,128]{1,0:T(8,128)(2,1)} %feat_hbm.1, bf16[4,128,128]{2,1,0:T(8,128)(2,1)} %bitcast.3, s32[1,16]{1,0:T(1,128)} %bitcast.5, s32[16,1,16]{2,1,0:T(1,128)} %cols_hbm.1, s32[16,1,16]{2,1,0:T(1,128)} %cols_hbm.1), custom_call_target="tpu_custom_call" | custom-call | tf_op jit(solution)/shard_map/pallas_call | solution.py:344
  92.2 0.0 copy-start
  92.2 1.6 %copy.8 = f32[256,128]{1,0:T(8,128)} copy(f32[256,128]{1,0:T(8,128)} %get-tuple-element.8) | data formatting | bytes 262144
  93.8 0.0 copy-done
  93.8 0.6 copy.9
Async XLA Ops:
  92.2 1.6 %copy-start = (f32[4,128]{1,0:T(4,128)S(1)}, f32[4,128]{1,0:T(4,128)}, u32[]{:S(2)}) copy-start(f32[4,128]{1,0:T(4,128)} %get-tuple-element.5) | copy-start | bytes 6148

commit v4 on v3

--- a/solution.py
+++ b/solution.py
@@ -53,9 +53,6 @@
     sub8 = lax.broadcasted_iota(jnp.int32, (8, TILE), 0)
     lane16 = lax.broadcasted_iota(jnp.int32, (ROWS, TILE), 1)
 
-    def peer_f(k):
-        return lax.rem(me_f + k, NF)
-
     def peer_c(k):
         return lax.rem(me_c + k, NC)
 
@@ -77,11 +74,12 @@
     cols_copy.start()
 
     barrier = pltpu.get_barrier_semaphore()
-    for k in range(1, NF):
-        pl.semaphore_signal(barrier, inc=1, device_id={"frames": peer_f(k)}, device_id_type=MESH)
+    for k in (2, 1, 3):
+        for where in (lax.rem(x + k, 4) * 4 + z, x * 4 + lax.rem(z + k, 4)):
+            pl.semaphore_signal(barrier, inc=1, device_id={"frames": where}, device_id_type=MESH)
     for k in range(1, NC):
         pl.semaphore_signal(barrier, inc=1, device_id={"codes": peer_c(k)}, device_id_type=MESH)
-    pl.semaphore_wait(barrier, NF - 1 + NC - 1)
+    pl.semaphore_wait(barrier, 6 + NC - 1)
     code_copy.wait()
 
     def at(h, first, second):
@@ -130,9 +128,10 @@
     for t in range(OWN):
         own = book[me_f * OWN + t].astype(F32)
         scales.append(lax.rsqrt(jnp.sum((own * own).T, axis=0, keepdims=True) / TILE + EPS))
-    cs[share(me_f), :] = jnp.concatenate(scales + [jnp.ones((PAD - OWN, TILE), F32)], axis=0)
-    for k in range(1, NF):
-        send(cs.at[share(me_f)], cs.at[share(me_f)], cs_s, cs_r, {"frames": peer_f(k)})
+    own_cs = cs.at[share(z * 4 + x)]
+    own_cs[...] = jnp.concatenate(scales + [jnp.ones((PAD - OWN, TILE), F32)], axis=0)
+    for k in (2, 1, 3):
+        send(own_cs, own_cs, cs_s.at[0], cs_r.at[0], {"frames": at(0, k, 0)})
 
     for h in range(2):
         first_forwards(h)
@@ -162,6 +161,10 @@
     for h in range(2):
         second_forwards(h, 1)
         second_forwards(h, 3)
+    drain(cs.at[pl.ds(0, 3 * PAD)], cs_r.at[0])
+    line_cs = cs.at[pl.ds(pl.multiple_of(z * 4 * PAD, 4 * PAD), 4 * PAD)]
+    for k in (2, 1, 3):
+        send(line_cs, line_cs, cs_s.at[1], cs_r.at[1], {"frames": at(0, 0, k)})
 
     count = jnp.zeros((ROWS, SLOTS), jnp.int32)
     for i in range(ROWS):
@@ -185,7 +188,10 @@
                 continue
             drain(chunk(h, j, 2, 0), book_r.at[h, 6 + j, 0])
             drain(chunk(h, j, 2, 1), book_r.at[h, 6 + j, 1])
-    drain(cs.at[pl.ds(0, (NF - 1) * PAD)], cs_r)
+    drain(cs.at[pl.ds(0, 3 * 4 * PAD)], cs_r.at[1])
+
+    def scale_row(c):
+        return (lax.rem(c // OWN, 4) * 4 + c // (4 * OWN)) * PAD + lax.rem(c, OWN)
 
     def build(i, _):
         a = feat[tile_rows(i), :]
@@ -195,7 +201,7 @@
             at2 = [cols_s[i, 0, s + j] for j in range(2)]
             words = jnp.concatenate([book[c] for c in at2], axis=0)
             scale = jnp.concatenate(
-                [cs[pl.ds((c // OWN) * PAD + lax.rem(c, OWN), 1), :] for c in at2], axis=1)
+                [cs[pl.ds(scale_row(c), 1), :] for c in at2], axis=1)
             p = lax.dot_general(a, words, NT, preferred_element_type=F32)
             k = jnp.exp2(p * f * scale)
             exact[tile_rows(i), s * TILE:(s + 2) * TILE] = k
@@ -268,9 +274,6 @@
         return 0
 
     lax.fori_loop(0, ITERS, sweep, 0)
-    log_out[...] = jnp.log(jnp.concatenate(
-        [v_ref[pl.ds(me_f * OWN + t, 1), :] for t in range(OWN)], axis=0))
-
     def mix(c, dst):
         def one(j, _):
             i = 2 * c + j
@@ -313,17 +316,10 @@
 
     lax.fori_loop(0, 4, mix_step, 0)
     join(3)
-    for k in range(3):
-        drain(yrx.at[k], y_r.at[k])
-    for j in range(2):
-        rows = slice(j * TILE, (j + 1) * TILE)
-        acc = mine[3, rows, :]
-        for k in range(3):
-            acc = acc + yrx[k, rows, :]
-        q_out[rows, :] = acc * column(u_ref[pl.ds(2 * me_c + j, 1), :])
 
     drain(book.at[pl.ds(0, 60)], book_s)
-    drain(cs.at[pl.ds(0, (NF - 1) * PAD)], cs_s)
+    drain(cs.at[pl.ds(0, 3 * PAD)], cs_s.at[0])
+    drain(cs.at[pl.ds(0, 3 * 4 * PAD)], cs_s.at[1])
     for it in range(ITERS):
         for g in range(2):
             drain(rowrx.at[it, g, pl.ds(0, NC - 1)], row_s.at[it, g])
@@ -332,6 +328,21 @@
                 drain(sums.at[it, stage, h, pl.ds(0, 3)], col_s.at[it, stage, h])
     for k in range(4):
         drain(tosib.at[k], sib_s.at[k])
+    log_out[...] = jnp.log(jnp.concatenate(
+        [v_ref[pl.ds(me_f * OWN + t, 1), :] for t in range(OWN)], axis=0))
+    scale = [column(u_ref[pl.ds(2 * me_c + j, 1), :]) for j in range(2)]
+    for j in range(2):
+        rows = slice(j * TILE, (j + 1) * TILE)
+        mine[3, rows, :] = mine[3, rows, :] * scale[j]
+    for k in range(3):
+        drain(yrx.at[k], y_r.at[k])
+    for j in range(2):
+        rows = slice(j * TILE, (j + 1) * TILE)
+        acc = yrx[0, rows, :]
+        for k in range(1, 3):
+            acc = acc + yrx[k, rows, :]
+        q_out[rows, :] = mine[3, rows, :] + acc * scale[j]
+
     for k in range(3):
         drain(mine.at[k], y_s.at[k])
 
@@ -368,7 +379,7 @@
             pltpu.VMEM((4, 2 * TILE, TILE), F32),
             pltpu.VMEM((4, 2 * TILE, TILE), F32),
             pltpu.VMEM((3, 2 * TILE, TILE), F32),
-            dma, dma, dma, dma, dma((2, 11, 2)), dma, dma,
+            dma, dma, dma, dma, dma((2, 11, 2)), dma((2,)), dma((2,)),
             dma((ITERS, 2)), dma((ITERS, 2)), dma((ITERS, 2, 2)), dma((ITERS, 2, 2)),
             dma((4,)), dma((4,)), dma((4,)), dma((4,)),
         ],

time: 94.5 us -> 93.9 us (level)
  no operation moved by 1% of the time
where the time goes in v4:
time: 93.9 us; the launch traced here: 93.8 us
  Pallas kernels  91 us (97%)
  local copies, waits for them, and re-layouts  2.15 us (2%)
    pallas_call x1, Pallas kernels, per_device(): pl.pallas_call(functools.partial(kernel, target), out_shape=(jax.ShapeDty...  91 us
    unnamed x4, local copies, waits for them, and re-layouts  2.15 us

profile of v4, /device:TPU:1, one launch (start us, length us, event | category | flops | bytes accessed | tf_op | source)
XLA Modules:
  0.0 93.8 jit_solution(11561474758323441500)
XLA Ops:
  0.6 91.0 %shard_map.59 = (f32[256,128]{1,0:T(8,128)}, f32[4,128]{1,0:T(4,128)}) custom-call(bf16[2048,128]{1,0:T(8,128)(2,1)} %feat_hbm.1, bf16[4,128,128]{2,1,0:T(8,128)(2,1)} %bitcast.3, s32[1,16]{1,0:T(1,128)} %bitcast.5, s32[16,1,16]{2,1,0:T(1,128)} %cols_hbm.1, s32[16,1,16]{2,1,0:T(1,128)} %cols_hbm.1), custom_call_target="tpu_custom_call" | custom-call | tf_op jit(solution)/shard_map/pallas_call | solution.py:355
  91.6 0.0 copy-start
  91.6 1.6 %copy.8 = f32[256,128]{1,0:T(8,128)} copy(f32[256,128]{1,0:T(8,128)} %get-tuple-element.8) | data formatting | bytes 262144
  93.2 0.0 copy-done
  93.2 0.6 copy.9
Async XLA Ops:
  91.6 1.6 %copy-start = (f32[4,128]{1,0:T(4,128)S(1)}, f32[4,128]{1,0:T(4,128)}, u32[]{:S(2)}) copy-start(f32[4,128]{1,0:T(4,128)} %get-tuple-element.5) | copy-start | bytes 6148

commit v5 on v4

--- a/solution.py
+++ b/solution.py
@@ -128,10 +128,10 @@
     for t in range(OWN):
         own = book[me_f * OWN + t].astype(F32)
         scales.append(lax.rsqrt(jnp.sum((own * own).T, axis=0, keepdims=True) / TILE + EPS))
-    own_cs = cs.at[share(z * 4 + x)]
+    own_cs = cs.at[share(me_f)]
     own_cs[...] = jnp.concatenate(scales + [jnp.ones((PAD - OWN, TILE), F32)], axis=0)
     for k in (2, 1, 3):
-        send(own_cs, own_cs, cs_s.at[0], cs_r.at[0], {"frames": at(0, k, 0)})
+        send(own_cs, own_cs, cs_s.at[0], cs_r.at[0], {"frames": at(0, 0, k)})
 
     for h in range(2):
         first_forwards(h)
@@ -162,9 +162,9 @@
         second_forwards(h, 1)
         second_forwards(h, 3)
     drain(cs.at[pl.ds(0, 3 * PAD)], cs_r.at[0])
-    line_cs = cs.at[pl.ds(pl.multiple_of(z * 4 * PAD, 4 * PAD), 4 * PAD)]
+    line_cs = cs.at[pl.ds(pl.multiple_of(x * 4 * PAD, 4 * PAD), 4 * PAD)]
     for k in (2, 1, 3):
-        send(line_cs, line_cs, cs_s.at[1], cs_r.at[1], {"frames": at(0, 0, k)})
+        send(line_cs, line_cs, cs_s.at[1], cs_r.at[1], {"frames": at(0, k, 0)})
 
     count = jnp.zeros((ROWS, SLOTS), jnp.int32)
     for i in range(ROWS):
@@ -191,7 +191,7 @@
     drain(cs.at[pl.ds(0, 3 * 4 * PAD)], cs_r.at[1])
 
     def scale_row(c):
-        return (lax.rem(c // OWN, 4) * 4 + c // (4 * OWN)) * PAD + lax.rem(c, OWN)
+        return c * (PAD // OWN) - lax.rem(c, OWN)
 
     def build(i, _):
         a = feat[tile_rows(i), :]

time: 93.9 us -> 93.3 us (level)
  no operation moved by 1% of the time
where the time goes in v5:
time: 93.3 us; the launch traced here: 93.1 us
  Pallas kernels  90.3 us (97%)
  local copies, waits for them, and re-layouts  2.15 us (2%)
    pallas_call x1, Pallas kernels, per_device(): pl.pallas_call(functools.partial(kernel, target), out_shape=(jax.ShapeDty...  90.3 us
    unnamed x4, local copies, waits for them, and re-layouts  2.15 us

profile of v5, /device:TPU:1, one launch (start us, length us, event | category | flops | bytes accessed | tf_op | source)
XLA Modules:
  0.0 93.1 jit_solution(7674265639036050943)
XLA Ops:
  0.6 90.3 %shard_map.59 = (f32[256,128]{1,0:T(8,128)}, f32[4,128]{1,0:T(4,128)}) custom-call(bf16[2048,128]{1,0:T(8,128)(2,1)} %feat_hbm.1, bf16[4,128,128]{2,1,0:T(8,128)(2,1)} %bitcast.3, s32[1,16]{1,0:T(1,128)} %bitcast.5, s32[16,1,16]{2,1,0:T(1,128)} %cols_hbm.1, s32[16,1,16]{2,1,0:T(1,128)} %cols_hbm.1), custom_call_target="tpu_custom_call" | custom-call | tf_op jit(solution)/shard_map/pallas_call | solution.py:355
  90.9 0.0 copy-start
  91.0 1.6 %copy.8 = f32[256,128]{1,0:T(8,128)} copy(f32[256,128]{1,0:T(8,128)} %get-tuple-element.8) | data formatting | bytes 262144
  92.5 0.0 copy-done
  92.5 0.6 copy.9
Async XLA Ops:
  90.9 1.6 %copy-start = (f32[4,128]{1,0:T(4,128)S(1)}, f32[4,128]{1,0:T(4,128)}, u32[]{:S(2)}) copy-start(f32[4,128]{1,0:T(4,128)} %get-tuple-element.5) | copy-start | bytes 6148
